TPU v7x, 32 devices: a whole 2x2x4 slice. The times are simulated.
32 devices in a mesh: chol: 4 (over y, x), pair: 8 (over z, core).
Axes of the slice: x: 2, y: 2, z: 4, core: 2. Of those that a mesh axis runs over, the one named last changes fastest.
Arguments:
- green: bfloat16 [2, 128, 147456], P(None, 'chol', 'pair'), may hold values from -6 to 6
- chol_rot: bfloat16 [147456, 1024], P('pair', 'chol'), may hold values from -0.015625 to 0.015625
Outputs:
- force_bias: float32 [2, 128, 1024], P(None, 'pair', 'chol')
All inputs are finite; a program needn't handle non-finite values.
Results may differ from a plain program's by a relative error of at most 0.0003.
Values may be sent and summed in bfloat16 or wider, within the bound.
A program may use at most 64 MiB of HBM per device.

v0:
```python
import jax
import jax.numpy as jnp
from jax import lax
from jax.sharding import PartitionSpec as P


def local(green, chol_rot):
    partial_value = jnp.einsum(
        "cwp,pg->wcg",
        lax.all_gather(green, "chol", axis=1, tiled=True),
        chol_rot,
        preferred_element_type=jnp.float32,
    )
    summed = lax.psum_scatter(partial_value, "pair", scatter_dimension=0, tiled=True)
    return jnp.transpose(summed, (1, 0, 2))


def solution(mesh):
    return jax.shard_map(
        local,
        mesh=mesh,
        in_specs=(P(None, "chol", "pair"), P("pair", "chol")),
        out_specs=P(None, "pair", "chol"),
        check_vma=False,
    )
```

profile of v0, /device:TPU:7, one launch (start us, length us, event | category | flops | bytes accessed | tf_op | source)
XLA Modules:
  0.0 179.6 jit_solution(14260340009630837000)
XLA Ops:
  6.5 0.0 all-gather.2.cloned.1.call-start
  6.5 0.7 all-gather.2.cloned.1.call-update
  7.3 0.0 copy-start
  7.3 0.0 all-reduce.3.cloned.1.call-start
  7.3 98.5 %all-gather.2.cloned.1.call-done = bf16[2,128,18432]{2,1,0:T(8,128)(2,1)} async-done(((bf16[2,32,18432]{2,1,0:T(8,128)(2,1)}), bf16[2,128,18432]{2,1,0:T(8,128)(2,1)}) %all-gather.2.cloned.1.call-update) | async-done | bytes 9437200 | tf_op jit(solution)/shard_map/all_gather | solution.py:10
  105.8 10.4 %fusion.2 = f32[128,2,256]{0,2,1:T(8,128)S(1)} fusion(bf16[2,128,18432]{2,1,0:T(8,128)(2,1)} %all-gather.2.cloned.1.call-done, bf16[18432,256]{1,0:T(8,128)(2,1)} %param.3), kind=kOutput, calls=%fused_computation.2 | convolution fusion | flops 2415919104 | bytes 19136512 | tf_op jit(solution)/shard_map/cwp,pg->wcg/dot_general | solution.py:8
  116.2 0.8 copy.6
  117.1 0.0 all-reduce.3.cloned.1.call-update
  117.1 0.0 copy-done
  117.1 0.6 dynamic-slice
  118.4 53.0 %all-reduce.3.cloned.1.call-done = f32[128,2,256]{2,1,0:T(2,128)} async-done(((f32[128,2,256]{2,1,0:T(2,128)}), f32[128,2,256]{2,1,0:T(2,128)}) %all-reduce.3.cloned.1.call-update) | async-done | bytes 262160
  171.4 0.8 dynamic-slice_bitcast_fusion
  172.1 0.6 copy.7
Async XLA Ops:
  6.5 99.3 %all-gather.2.cloned.1.call-start = ((), (), s32[]{:S(2)}) async-start(), calls=%async_computation | async-start | bytes 11796480 | tf_op jit(solution)/shard_map/all_gather | solution.py:10
  7.3 109.9 %copy-start = (u32[32]{0:T(128)S(1)}, u32[32]{0:T(128)}, u32[]{:S(2)}) copy-start(u32[32]{0:T(128)} %constant.2) | copy-start | bytes 388
  7.3 164.1 %all-reduce.3.cloned.1.call-start = ((), (), s32[]{:S(2)}) async-start(), calls=%async_computation.1 | async-start | bytes 524288
Sparse Core Ops, SparseCore 0:
  9.2 96.5 all-gather.1
  117.2 54.1 all-reduce.2
where the time goes:
time: 183 us; the launch traced here: 180 us
  waiting for transfers between devices  152 us (83%)
  between operations  14.1 us (8%)
  matrix products  10.4 us (6%)
  local copies, waits for them, and re-layouts  2.81 us (2%)
    all_gather x1, waiting for transfers between devices, local(): lax.all_gather(green, 'chol', axis=1, tiled=True)  98.5 us
    unnamed x3, waiting for transfers between devices  53.7 us
    dot_general x1, matrix products, local(): jnp.einsum('cwp,pg->wcg', lax.all_gather(green, 'chol', axis=1, tiled=Tru...  10.4 us
  transfers between devices with their start and end apart: 2, of which 2 were waited for; matrix products, arithmetic and copies ran while one was open for 0% of the time, Pallas kernels for 0%

commit v1 on v0

--- a/solution.py
+++ b/solution.py
@@ -1,7 +1,210 @@
+import functools
+
 import jax
 import jax.numpy as jnp
 from jax import lax
+from jax.experimental import pallas as pl
+from jax.experimental.pallas import tpu as pltpu
 from jax.sharding import PartitionSpec as P
+
+MESH = pl.DeviceIdType.MESH
+CHUNKS = 18
+AHEAD = 4
+
+
+def kernel(pairs, green, chol, out, near, far, weights, total, staged, arrived,
+           own_sem, weight_sem, x_send, x_recv, y_send, y_recv, fx_send, fy_send, far_recv, sum_send, sum_recv):
+    n, width = near.shape[0], near.shape[-1]
+    half = n // 2
+    share = out.shape[1]
+    per_block = green.shape[1] // share
+    i, j = lax.axis_index("chol"), lax.axis_index("pair")
+    x, y = lax.rem(i, 2), i // 2
+    across, along = i + 1 - 2 * x, i + 2 - 4 * y
+    blocks = (i, across, along, 3 - i)
+
+    barrier = pltpu.get_barrier_semaphore()
+    for to in (across, along):
+        pl.semaphore_signal(barrier, inc=1, device_id=(to, j), device_id_type=MESH)
+    for step in range(1, pairs):
+        pl.semaphore_signal(barrier, inc=1, device_id=(i, lax.rem(j + step, pairs)), device_id_type=MESH)
+
+    def columns(c):
+        return pl.ds(pl.multiple_of(c * width, width), width)
+
+    def own(c):
+        return pltpu.make_async_copy(green.at[:, :, columns(c)], near.at[c, 0], own_sem.at[c])
+
+    def weight(c):
+        return pltpu.make_async_copy(chol.at[columns(c), :], weights.at[c], weight_sem.at[c])
+
+    def to_x(c):
+        return pltpu.make_async_remote_copy(green.at[:, :, columns(c)], near.at[c, 1], x_send.at[c], x_recv.at[c],
+                                            device_id=(across, j), device_id_type=MESH)
+
+    def to_y(c):
+        return pltpu.make_async_remote_copy(green.at[:, :, columns(c)], near.at[c, 2], y_send.at[c], y_recv.at[c],
+                                            device_id=(along, j), device_id_type=MESH)
+
+    def on_x(k):
+        return pltpu.make_async_remote_copy(near.at[2 * k, 2], far.at[2 * k], fx_send.at[k], far_recv.at[2 * k],
+                                            device_id=(across, j), device_id_type=MESH)
+
+    def on_y(k):
+        return pltpu.make_async_remote_copy(near.at[2 * k + 1, 1], far.at[2 * k + 1], fy_send.at[k],
+                                            far_recv.at[2 * k + 1], device_id=(along, j), device_id_type=MESH)
+
+    def loop(low, high, body):
+        lax.fori_loop(low, high, lambda s, _: (body(s), 0)[1], 0)
+
+    def start_local(c):
+        own(c).start()
+        weight(c).start()
+
+    def start_own(c):
+        to_x(c).start()
+        to_y(c).start()
+
+    def start_on(k):
+        on_x(k).start()
+        on_y(k).start()
+
+    pl.semaphore_wait(barrier, pairs + 1)
+    loop(0, AHEAD, start_own)
+    loop(0, n, start_local)
+    total[...] = jnp.zeros_like(total)
+
+    def first(c):
+        own(c).wait()
+        weight(c).wait()
+        rows = near[c].reshape(-1, width)
+        total[: rows.shape[0]] += jnp.dot(rows, weights[c], preferred_element_type=jnp.float32)
+
+    def arrive(c):
+        to_x(c).wait_recv()
+        to_y(c).wait_recv()
+
+    def phase_a(s):
+        arrive(s)
+        start_own(s + AHEAD)
+        first(s)
+
+    def phase_b(s):
+        arrive(s)
+        start_on(s + AHEAD - n)
+        first(s)
+
+    loop(0, n - AHEAD, phase_a)
+    loop(n - AHEAD, n, phase_b)
+
+    block_rows = 2 * green.shape[1]
+
+    def sum_copy(slot, h):
+        to = blocks[slot] * per_block + h
+        return to, pltpu.make_async_remote_copy(
+            staged.at[slot, h], arrived.at[j], sum_send.at[slot, h], sum_recv.at[j],
+            device_id=(i, to), device_id_type=MESH)
+
+    def send_sums(slot):
+        part = total[slot * block_rows : (slot + 1) * block_rows].reshape(2, green.shape[1], -1)
+        for h in range(per_block):
+            staged[slot, h] = part[:, h * share : (h + 1) * share]
+            to, copy = sum_copy(slot, h)
+
+            @pl.when(to != j)
+            def _():
+                copy.start()
+
+            @pl.when(to == j)
+            def _():
+                arrived[j] = staged[slot, h]
+
+    for slot in range(3):
+        send_sums(slot)
+
+    def last(k):
+        on_x(k).wait_recv()
+        on_y(k).wait_recv()
+
+    def multiply_last(k):
+        part = jnp.dot(far[2 * k].reshape(-1, width), weights[2 * k], preferred_element_type=jnp.float32)
+        part += jnp.dot(far[2 * k + 1].reshape(-1, width), weights[2 * k + 1], preferred_element_type=jnp.float32)
+        total[3 * block_rows :] += part
+
+    def phase_c(k):
+        last(k)
+        start_on(k + AHEAD)
+        multiply_last(k)
+
+    def phase_d(k):
+        last(k)
+        multiply_last(k)
+
+    loop(0, half - AHEAD, phase_c)
+    loop(half - AHEAD, half, phase_d)
+    send_sums(3)
+
+    for slot in range(4):
+        for h in range(per_block):
+            to, copy = sum_copy(slot, h)
+
+            @pl.when(to != j)
+            def _():
+                copy.wait_send()
+
+    def end_own(c):
+        to_x(c).wait_send()
+        to_y(c).wait_send()
+
+    def end_on(k):
+        on_x(k).wait_send()
+        on_y(k).wait_send()
+
+    loop(0, n, end_own)
+    loop(0, half, end_on)
+
+    for source in range(pairs):
+        @pl.when(source != j)
+        def _():
+            pltpu.make_async_remote_copy(staged.at[0, 0], arrived.at[source], sum_send.at[0, 0], sum_recv.at[source],
+                                         device_id=(i, source), device_id_type=MESH).wait_recv()
+
+    result = arrived[0]
+    for source in range(1, pairs):
+        result += arrived[source]
+    out[...] = result
+
+
+def local_kernel(pairs, green, chol_rot):
+    parts, walkers, depth = green.shape
+    columns = chol_rot.shape[1]
+    n = CHUNKS
+    width = depth // n
+    share = 4 * walkers // pairs
+    dma = pltpu.SemaphoreType.DMA
+    return pl.pallas_call(
+        functools.partial(kernel, pairs),
+        out_shape=jax.ShapeDtypeStruct((parts, share, columns), jnp.float32),
+        in_specs=[pl.BlockSpec(memory_space=pl.ANY)] * 2,
+        out_specs=pl.BlockSpec(memory_space=pltpu.VMEM),
+        scratch_shapes=[
+            pltpu.VMEM((n, 3, parts, walkers, width), jnp.bfloat16),
+            pltpu.VMEM((n, parts, walkers, width), jnp.bfloat16),
+            pltpu.VMEM((n, width, columns), jnp.bfloat16),
+            pltpu.VMEM((4 * parts * walkers, columns), jnp.float32),
+            pltpu.VMEM((4, walkers // share, parts, share, columns), jnp.float32),
+            pltpu.VMEM((pairs, parts, share, columns), jnp.float32),
+            dma((n,)), dma((n,)), dma((n,)), dma((n,)), dma((n,)), dma((n,)),
+            dma((n // 2,)), dma((n // 2,)), dma((n,)),
+            dma((4, walkers // share)), dma((pairs,)),
+        ],
+        compiler_params=pltpu.CompilerParams(
+            collective_id=0, has_side_effects=True, vmem_limit_bytes=56 * 1024 * 1024
+        ),
+        cost_estimate=pl.CostEstimate(
+            flops=2 * 4 * parts * walkers * depth * columns,
+            bytes_accessed=2 * depth * (columns + 3 * parts * walkers), transcendentals=0),
+    )(green, chol_rot)
 
 
 def local(green, chol_rot):
@@ -16,8 +219,10 @@
 
 
 def solution(mesh):
+    chols, pairs = mesh.shape["chol"], mesh.shape["pair"]
+    plane = chols == 4 and pairs % 4 == 0
     return jax.shard_map(
-        local,
+        functools.partial(local_kernel, pairs) if plane else local,
         mesh=mesh,
         in_specs=(P(None, "chol", "pair"), P("pair", "chol")),
         out_specs=P(None, "pair", "chol"),

time: 183 us -> 90 us (0.49); the launches traced: 180 us -> 89.9 us
  waiting for transfers between devices: 152 us -> 0 us
  Pallas kernels: 0 us -> 88.5 us
  between operations: 14.1 us -> 0.01 us
  matrix products: 10.4 us -> 0 us
    all_gather x1 -> x0, waiting for transfers between devices: 98.5 us -> none  [local(): lax.all_gather(green, 'chol', axis=1, tiled=True)]
    pallas_call x0 -> x1, Pallas kernels: none -> 88.5 us  [local_kernel(): pl.pallas_call(functools.partial(kernel, pairs), out_shape=jax.ShapeDtype...]
    unnamed x3 -> x0, waiting for transfers between devices: 53.7 us -> none
    dot_general x1 -> x0, matrix products: 10.4 us -> none  [local(): jnp.einsum('cwp,pg->wcg', lax.all_gather(green, 'chol', axis=1, tiled=Tru...]
    transpose x3 -> x0, local copies, waits for them, and re-layouts: 2.21 us -> none  [the longest x2 1.38 us: local(): return jnp.transpose(summed, (1, 0, 2))]
  transfers between devices with their start and end apart: 2 -> 0, of which waited for: 2 -> 0; matrix products, arithmetic and copies ran while one was open for 0% -> 0% of each run, Pallas kernels for 0% -> 0%
where the time goes in v1:
time: 90 us; the launch traced here: 89.9 us
  Pallas kernels  88.5 us (98%)
  local copies, waits for them, and re-layouts  1.38 us (2%)
    pallas_call x1, Pallas kernels, local_kernel(): pl.pallas_call(functools.partial(kernel, pairs), out_shape=jax.ShapeDtype...  88.5 us

profile of v1, /device:TPU:7, one launch (start us, length us, event | category | flops | bytes accessed | tf_op | source)
XLA Modules:
  0.0 89.9 jit_solution(11228862885347714617)
XLA Ops:
  0.0 88.5 %shard_map.28 = f32[2,16,256]{2,1,0:T(8,128)} custom-call(bf16[2,32,18432]{2,1,0:T(8,128)(2,1)} %green.1, bf16[18432,256]{1,0:T(8,128)(2,1)} %chol.1), custom_call_target="tpu_custom_call" | custom-call | flops 2415919104 | bytes 16515072 | tf_op jit(solution)/shard_map/pallas_call | solution.py:185
  88.5 1.4 %copy.4 = f32[2,16,256]{2,1,0:T(8,128)} copy(f32[2,16,256]{2,1,0:T(8,128)} %shard_map.28) | data formatting | bytes 65536

commit v2 on v1

--- a/solution.py
+++ b/solution.py
@@ -13,7 +13,7 @@
 
 
 def kernel(pairs, green, chol, out, near, far, weights, total, staged, arrived,
-           own_sem, weight_sem, x_send, x_recv, y_send, y_recv, fx_send, fy_send, far_recv, sum_send, sum_recv):
+           own_sem, weight_sem, x_send, x_recv, y_send, y_recv, fx_send, fy_send, far_recv, sum_send, sum_recv, up, down):
     n, width = near.shape[0], near.shape[-1]
     half = n // 2
     share = out.shape[1]
@@ -26,8 +26,16 @@
     barrier = pltpu.get_barrier_semaphore()
     for to in (across, along):
         pl.semaphore_signal(barrier, inc=1, device_id=(to, j), device_id_type=MESH)
-    for step in range(1, pairs):
-        pl.semaphore_signal(barrier, inc=1, device_id=(i, lax.rem(j + step, pairs)), device_id_type=MESH)
+    pl.semaphore_signal(barrier, inc=1, device_id=(i, j + 1 - 2 * lax.rem(j, 2)), device_id_type=MESH)
+    has_below, has_above = j >= 2, j < pairs - 2
+
+    @pl.when(has_below)
+    def _():
+        pl.semaphore_signal(barrier, inc=1, device_id=(i, j - 2), device_id_type=MESH)
+
+    @pl.when(has_above)
+    def _():
+        pl.semaphore_signal(barrier, inc=1, device_id=(i, j + 2), device_id_type=MESH)
 
     def columns(c):
         return pl.ds(pl.multiple_of(c * width, width), width)
@@ -69,10 +77,19 @@
         on_x(k).start()
         on_y(k).start()
 
-    pl.semaphore_wait(barrier, pairs + 1)
+    pl.semaphore_wait(barrier, 4 + (j + pairs - 2) // pairs - (j + 2) // pairs)
     loop(0, AHEAD, start_own)
     loop(0, n, start_local)
     total[...] = jnp.zeros_like(total)
+
+    for has_from, has_to, to, token in ((has_below, has_above, j + 2, up), (has_above, has_below, j - 2, down)):
+        @pl.when(has_from)
+        def _():
+            pl.semaphore_wait(token, 1)
+
+        @pl.when(has_to)
+        def _():
+            pl.semaphore_signal(token, inc=1, device_id=(i, to), device_id_type=MESH)
 
     def first(c):
         own(c).wait()
@@ -197,6 +214,7 @@
             dma((n,)), dma((n,)), dma((n,)), dma((n,)), dma((n,)), dma((n,)),
             dma((n // 2,)), dma((n // 2,)), dma((n,)),
             dma((4, walkers // share)), dma((pairs,)),
+            pltpu.SemaphoreType.REGULAR, pltpu.SemaphoreType.REGULAR,
         ],
         compiler_params=pltpu.CompilerParams(
             collective_id=0, has_side_effects=True, vmem_limit_bytes=56 * 1024 * 1024

time: 90 us -> 88.4 us (0.982)
  Pallas kernels: 88.5 us -> 86.9 us
    pallas_call x1, Pallas kernels: 88.5 us -> 86.9 us  [local_kernel(): pl.pallas_call(functools.partial(kernel, pairs), out_shape=jax.ShapeDtype...]
where the time goes in v2:
time: 88.4 us; the launch traced here: 88.2 us
  Pallas kernels  86.9 us (98%)
  local copies, waits for them, and re-layouts  1.38 us (2%)
    pallas_call x1, Pallas kernels, local_kernel(): pl.pallas_call(functools.partial(kernel, pairs), out_shape=jax.ShapeDtype...  86.9 us

profile of v2, /device:TPU:7, one launch (start us, length us, event | category | flops | bytes accessed | tf_op | source)
XLA Modules:
  0.0 88.2 jit_solution(10944652686732939319)
XLA Ops:
  0.0 86.9 %shard_map.28 = f32[2,16,256]{2,1,0:T(8,128)} custom-call(bf16[2,32,18432]{2,1,0:T(8,128)(2,1)} %green.1, bf16[18432,256]{1,0:T(8,128)(2,1)} %chol.1), custom_call_target="tpu_custom_call" | custom-call | flops 2415919104 | bytes 16515072 | tf_op jit(solution)/shard_map/pallas_call | solution.py:202
  86.9 1.4 %copy.4 = f32[2,16,256]{2,1,0:T(8,128)} copy(f32[2,16,256]{2,1,0:T(8,128)} %shard_map.28) | data formatting | bytes 65536

commit v3 on v2

--- a/solution.py
+++ b/solution.py
@@ -8,7 +8,7 @@
 from jax.sharding import PartitionSpec as P
 
 MESH = pl.DeviceIdType.MESH
-CHUNKS = 18
+CHUNKS = 12
 AHEAD = 4
 
 
@@ -41,25 +41,24 @@
         return pl.ds(pl.multiple_of(c * width, width), width)
 
     def own(c):
-        return pltpu.make_async_copy(green.at[:, :, columns(c)], near.at[c, 0], own_sem.at[c])
-
-    def weight(c):
-        return pltpu.make_async_copy(chol.at[columns(c), :], weights.at[c], weight_sem.at[c])
+        return pltpu.make_async_copy(green.at[:, :, columns(c)], near.at[c, 0], own_sem)
+
+    weight = pltpu.make_async_copy(chol, weights, weight_sem)
 
     def to_x(c):
-        return pltpu.make_async_remote_copy(green.at[:, :, columns(c)], near.at[c, 1], x_send.at[c], x_recv.at[c],
+        return pltpu.make_async_remote_copy(green.at[:, :, columns(c)], near.at[c, 1], x_send, x_recv.at[c],
                                             device_id=(across, j), device_id_type=MESH)
 
     def to_y(c):
-        return pltpu.make_async_remote_copy(green.at[:, :, columns(c)], near.at[c, 2], y_send.at[c], y_recv.at[c],
+        return pltpu.make_async_remote_copy(green.at[:, :, columns(c)], near.at[c, 2], y_send, y_recv.at[c],
                                             device_id=(along, j), device_id_type=MESH)
 
     def on_x(k):
-        return pltpu.make_async_remote_copy(near.at[2 * k, 2], far.at[2 * k], fx_send.at[k], far_recv.at[2 * k],
+        return pltpu.make_async_remote_copy(near.at[2 * k, 2], far.at[2 * k], fx_send, far_recv.at[2 * k],
                                             device_id=(across, j), device_id_type=MESH)
 
     def on_y(k):
-        return pltpu.make_async_remote_copy(near.at[2 * k + 1, 1], far.at[2 * k + 1], fy_send.at[k],
+        return pltpu.make_async_remote_copy(near.at[2 * k + 1, 1], far.at[2 * k + 1], fy_send,
                                             far_recv.at[2 * k + 1], device_id=(along, j), device_id_type=MESH)
 
     def loop(low, high, body):
@@ -67,7 +66,6 @@
 
     def start_local(c):
         own(c).start()
-        weight(c).start()
 
     def start_own(c):
         to_x(c).start()
@@ -79,6 +77,7 @@
 
     pl.semaphore_wait(barrier, 4 + (j + pairs - 2) // pairs - (j + 2) // pairs)
     loop(0, AHEAD, start_own)
+    weight.start()
     loop(0, n, start_local)
     total[...] = jnp.zeros_like(total)
 
@@ -92,8 +91,6 @@
             pl.semaphore_signal(token, inc=1, device_id=(i, to), device_id_type=MESH)
 
     def first(c):
-        own(c).wait()
-        weight(c).wait()
         rows = near[c].reshape(-1, width)
         total[: rows.shape[0]] += jnp.dot(rows, weights[c], preferred_element_type=jnp.float32)
 
@@ -111,6 +108,8 @@
         start_on(s + AHEAD - n)
         first(s)
 
+    pltpu.make_async_copy(near.at[:, 0], near.at[:, 0], own_sem).wait()
+    weight.wait()
     loop(0, n - AHEAD, phase_a)
     loop(n - AHEAD, n, phase_b)
 
@@ -139,6 +138,10 @@
     for slot in range(3):
         send_sums(slot)
 
+    def end_sends(count, send):
+        sent = near.at[pl.ds(0, count), 1]
+        pltpu.make_async_remote_copy(sent, sent, send, x_recv.at[0], device_id=(across, j), device_id_type=MESH).wait_send()
+
     def last(k):
         on_x(k).wait_recv()
         on_y(k).wait_recv()
@@ -158,6 +161,8 @@
         multiply_last(k)
 
     loop(0, half - AHEAD, phase_c)
+    end_sends(n, x_send)
+    end_sends(n, y_send)
     loop(half - AHEAD, half, phase_d)
     send_sums(3)
 
@@ -169,25 +174,14 @@
             def _():
                 copy.wait_send()
 
-    def end_own(c):
-        to_x(c).wait_send()
-        to_y(c).wait_send()
-
-    def end_on(k):
-        on_x(k).wait_send()
-        on_y(k).wait_send()
-
-    loop(0, n, end_own)
-    loop(0, half, end_on)
-
-    for source in range(pairs):
-        @pl.when(source != j)
-        def _():
-            pltpu.make_async_remote_copy(staged.at[0, 0], arrived.at[source], sum_send.at[0, 0], sum_recv.at[source],
-                                         device_id=(i, source), device_id_type=MESH).wait_recv()
-
-    result = arrived[0]
-    for source in range(1, pairs):
+    end_sends(half, fx_send)
+    end_sends(half, fy_send)
+
+    result = arrived[j]
+    for step in range(1, pairs):
+        source = lax.rem(j + step, pairs)
+        pltpu.make_async_remote_copy(staged.at[0, 0], arrived.at[source], sum_send.at[0, 0], sum_recv.at[source],
+                                     device_id=(i, source), device_id_type=MESH).wait_recv()
         result += arrived[source]
     out[...] = result
 
@@ -211,8 +205,7 @@
             pltpu.VMEM((4 * parts * walkers, columns), jnp.float32),
             pltpu.VMEM((4, walkers // share, parts, share, columns), jnp.float32),
             pltpu.VMEM((pairs, parts, share, columns), jnp.float32),
-            dma((n,)), dma((n,)), dma((n,)), dma((n,)), dma((n,)), dma((n,)),
-            dma((n // 2,)), dma((n // 2,)), dma((n,)),
+            dma, dma, dma, dma((n,)), dma, dma((n,)), dma, dma, dma((n,)),
             dma((4, walkers // share)), dma((pairs,)),
             pltpu.SemaphoreType.REGULAR, pltpu.SemaphoreType.REGULAR,
         ],
@@ -222,7 +215,7 @@
         cost_estimate=pl.CostEstimate(
             flops=2 * 4 * parts * walkers * depth * columns,
             bytes_accessed=2 * depth * (columns + 3 * parts * walkers), transcendentals=0),
-    )(green, chol_rot)
+    )(green, chol_rot.reshape(n, width, columns))
 
 
 def local(green, chol_rot):

time: 88.4 us -> 87.6 us (level)
  Pallas kernels: 86.9 us -> 86 us
where the time goes in v3:
time: 87.6 us; the launch traced here: 87.4 us
  Pallas kernels  86 us (98%)
  local copies, waits for them, and re-layouts  1.38 us (2%)
    pallas_call x1, Pallas kernels, local_kernel(): pl.pallas_call(functools.partial(kernel, pairs), out_shape=jax.ShapeDtype...  86 us

profile of v3, /device:TPU:7, one launch (start us, length us, event | category | flops | bytes accessed | tf_op | source)
XLA Modules:
  0.0 87.4 jit_solution(16115716624837660602)
XLA Ops:
  0.0 86.0 %shard_map.28 = f32[2,16,256]{2,1,0:T(8,128)} custom-call(bf16[2,32,18432]{2,1,0:T(8,128)(2,1)} %green.1, bf16[12,1536,256]{2,1,0:T(8,128)(2,1)} %bitcast.1), custom_call_target="tpu_custom_call" | custom-call | flops 2415919104 | bytes 16515072 | tf_op jit(solution)/shard_map/pallas_call | solution.py:196
  86.0 1.4 %copy.4 = f32[2,16,256]{2,1,0:T(8,128)} copy(f32[2,16,256]{2,1,0:T(8,128)} %shard_map.28) | data formatting | bytes 65536

commit v4 on v3

--- a/solution.py
+++ b/solution.py
@@ -12,11 +12,11 @@
 AHEAD = 4
 
 
-def kernel(pairs, green, chol, out, near, far, weights, total, staged, arrived,
-           own_sem, weight_sem, x_send, x_recv, y_send, y_recv, fx_send, fy_send, far_recv, sum_send, sum_recv, up, down):
+def kernel(pairs, green, chol, arrived, near, far, weights, total, staged,
+           own_sem, weight_sem, x_send, x_recv, y_send, y_recv, fx_send, fy_send, far_recv, sum_send, sum_recv, keep_sem, up, down):
     n, width = near.shape[0], near.shape[-1]
     half = n // 2
-    share = out.shape[1]
+    share = arrived.shape[2]
     per_block = green.shape[1] // share
     i, j = lax.axis_index("chol"), lax.axis_index("pair")
     x, y = lax.rem(i, 2), i // 2
@@ -133,7 +133,7 @@
 
             @pl.when(to == j)
             def _():
-                arrived[j] = staged[slot, h]
+                pltpu.make_async_copy(staged.at[slot, h], arrived.at[j], keep_sem).start()
 
     for slot in range(3):
         send_sums(slot)
@@ -174,16 +174,17 @@
             def _():
                 copy.wait_send()
 
+            @pl.when(to == j)
+            def _():
+                pltpu.make_async_copy(staged.at[slot, h], arrived.at[j], keep_sem).wait()
+
     end_sends(half, fx_send)
     end_sends(half, fy_send)
 
-    result = arrived[j]
     for step in range(1, pairs):
         source = lax.rem(j + step, pairs)
         pltpu.make_async_remote_copy(staged.at[0, 0], arrived.at[source], sum_send.at[0, 0], sum_recv.at[source],
                                      device_id=(i, source), device_id_type=MESH).wait_recv()
-        result += arrived[source]
-    out[...] = result
 
 
 def local_kernel(pairs, green, chol_rot):
@@ -193,20 +194,19 @@
     width = depth // n
     share = 4 * walkers // pairs
     dma = pltpu.SemaphoreType.DMA
-    return pl.pallas_call(
+    shares = pl.pallas_call(
         functools.partial(kernel, pairs),
-        out_shape=jax.ShapeDtypeStruct((parts, share, columns), jnp.float32),
+        out_shape=jax.ShapeDtypeStruct((pairs, parts, share, columns), jnp.float32),
         in_specs=[pl.BlockSpec(memory_space=pl.ANY)] * 2,
-        out_specs=pl.BlockSpec(memory_space=pltpu.VMEM),
+        out_specs=pl.BlockSpec(memory_space=pl.ANY),
         scratch_shapes=[
             pltpu.VMEM((n, 3, parts, walkers, width), jnp.bfloat16),
             pltpu.VMEM((n, parts, walkers, width), jnp.bfloat16),
             pltpu.VMEM((n, width, columns), jnp.bfloat16),
             pltpu.VMEM((4 * parts * walkers, columns), jnp.float32),
             pltpu.VMEM((4, walkers // share, parts, share, columns), jnp.float32),
-            pltpu.VMEM((pairs, parts, share, columns), jnp.float32),
             dma, dma, dma, dma((n,)), dma, dma((n,)), dma, dma, dma((n,)),
-            dma((4, walkers // share)), dma((pairs,)),
+            dma((4, walkers // share)), dma((pairs,)), dma,
             pltpu.SemaphoreType.REGULAR, pltpu.SemaphoreType.REGULAR,
         ],
         compiler_params=pltpu.CompilerParams(
@@ -216,6 +216,7 @@
             flops=2 * 4 * parts * walkers * depth * columns,
             bytes_accessed=2 * depth * (columns + 3 * parts * walkers), transcendentals=0),
     )(green, chol_rot.reshape(n, width, columns))
+    return jnp.sum(shares, axis=0)
 
 
 def local(green, chol_rot):

time: 87.6 us -> 87.3 us (level)
  other arithmetic: 0 us -> 1.59 us
  local copies, waits for them, and re-layouts: 1.38 us -> 0 us
    reduce_sum x0 -> x1, other arithmetic: none -> 1.59 us  [local_kernel(): return jnp.sum(shares, axis=0)]
    unnamed x1 -> x0, local copies, waits for them, and re-layouts: 1.38 us -> none
where the time goes in v4:
time: 87.3 us; the launch traced here: 87.1 us
  Pallas kernels  85.5 us (98%)
  other arithmetic  1.59 us (2%)
    pallas_call x1, Pallas kernels, local_kernel(): pl.pallas_call(functools.partial(kernel, pairs), out_shape=jax.ShapeDtype...  85.5 us

profile of v4, /device:TPU:7, one launch (start us, length us, event | category | flops | bytes accessed | tf_op | source)
XLA Modules:
  0.0 87.1 jit_solution(4848679177032933113)
XLA Ops:
  0.0 85.5 %shard_map.28 = f32[8,2,16,256]{3,2,1,0:T(8,128)} custom-call(bf16[2,32,18432]{2,1,0:T(8,128)(2,1)} %green.1, bf16[12,1536,256]{2,1,0:T(8,128)(2,1)} %bitcast.1), custom_call_target="tpu_custom_call" | custom-call | flops 2415919104 | bytes 16515072 | tf_op jit(solution)/shard_map/pallas_call | solution.py:197
  85.5 1.6 %reduce_sum.9 = f32[2,16,256]{2,1,0:T(8,128)} reduce(f32[8,2,16,256]{3,2,1,0:T(8,128)} %shard_map.28, f32[]{:T(128)} %constant.0.clone.1), dimensions={0}, to_apply=%region_0.0 | reduce | flops 57344 | bytes 294916 | tf_op jit(solution)/shard_map/reduce_sum | solution.py:219

commit v5 on v4

--- a/solution.py
+++ b/solution.py
@@ -8,7 +8,7 @@
 from jax.sharding import PartitionSpec as P
 
 MESH = pl.DeviceIdType.MESH
-CHUNKS = 12
+CHUNKS = 8
 AHEAD = 4
 
 

time: 87.3 us -> 87.3 us (level)
  no operation moved by 1% of the time
where the time goes in v5:
time: 87.3 us; the launch traced here: 87.2 us
  Pallas kernels  85.6 us (98%)
  other arithmetic  1.59 us (2%)
    pallas_call x1, Pallas kernels, local_kernel(): pl.pallas_call(functools.partial(kernel, pairs), out_shape=jax.ShapeDtype...  85.6 us

profile of v5, /device:TPU:7, one launch (start us, length us, event | category | flops | bytes accessed | tf_op | source)
XLA Modules:
  0.0 87.2 jit_solution(10566753009687008713)
XLA Ops:
  0.0 85.6 %shard_map.28 = f32[8,2,16,256]{3,2,1,0:T(8,128)} custom-call(bf16[2,32,18432]{2,1,0:T(8,128)(2,1)} %green.1, bf16[8,2304,256]{2,1,0:T(8,128)(2,1)} %bitcast.1), custom_call_target="tpu_custom_call" | custom-call | flops 2415919104 | bytes 16515072 | tf_op jit(solution)/shard_map/pallas_call | solution.py:197
  85.6 1.6 %reduce_sum.9 = f32[2,16,256]{2,1,0:T(8,128)} reduce(f32[8,2,16,256]{3,2,1,0:T(8,128)} %shard_map.28, f32[]{:T(128)} %constant.0.clone.1), dimensions={0}, to_apply=%region_0.0 | reduce | flops 57344 | bytes 294916 | tf_op jit(solution)/shard_map/reduce_sum | solution.py:219
